TPU v7x, 128 devices: a whole 4x4x4 slice. The times are simulated.
128 devices in a mesh: prow: 8 (over x_lo, z), pcol: 16 (over y, x_hi, core).
Axes of the slice: x: 4 (x_hi: 2, x_lo: 2; x = x_hi * 2 + x_lo), y: 4, z: 4, core: 2. Of those that a mesh axis runs over, the one named last changes fastest.
Arguments:
- values: float32 [12, 8, 4, 16, 256, 256], P(None, 'prow', None, 'pcol'), may hold values from -6 to 6
- pattern: int32 [12, 8, 4, 16], P(None, 'prow', None, 'pcol'), may hold values from 0 to 1
Outputs:
- factored: float32 [12, 8, 4, 16, 256, 256], P(None, 'prow', None, 'pcol')
All inputs are finite; a program needn't handle non-finite values.
Results may differ from a plain program's by a relative error of at most 0.0003.
Values sent between devices are 32-bit elements; how exact they have to be, the bound alone decides.
A program may use at most 128 MiB of HBM per device.

v0:
```python
import math

import jax
import jax.numpy as jnp
from jax import lax
from jax.sharding import Mesh
from jax.sharding import PartitionSpec as P

SWEEPS = 3
PROW = ("prow_0", "prow_1")


shift_coef = 5.0


def picked(value, axis, root):
    return lax.dynamic_index_in_dim(lax.all_gather(value, axis), root, 0, keepdims=False)


def rows_for(lines, peers):
    spare = -lines.shape[0] % peers
    if not spare:
        return lines
    return jnp.concatenate([lines, jnp.zeros((spare, *lines.shape[1:]), lines.dtype)])


def spread(value, axis, root):
    lines = jnp.where(lax.axis_index(axis) == root, value, jnp.zeros_like(value)).reshape(
        -1, *value.shape[1:][-1:]
    )
    padded = rows_for(lines, lax.axis_size(axis))
    own = lax.psum_scatter(padded, axis, scatter_dimension=0, tiled=True)
    return lax.all_gather(own, axis, axis=0, tiled=True)[: len(lines)].reshape(value.shape)


def broadcast_by_axis(value, axes, root):
    value = jnp.where(lax.axis_index(axes) == root, value, jnp.zeros_like(value))
    for axis in axes:
        value = lax.psum(value, axis)
    return value


def newton(block, shift):
    width = block.shape[0]
    eye = jnp.eye(width, dtype=jnp.float32)
    approx = eye / shift
    for step in range(SWEEPS):
        inner = jnp.dot(block, approx, precision=lax.Precision.HIGHEST)
        approx = jnp.dot(approx, 2.0 * eye - inner, precision=lax.Precision.HIGHEST)
    return approx


def spread_inverse(block, shift, root_row):
    return picked(newton(block, shift), PROW, root_row)


def apply_panel(blocks, rows_g, cols_g, mult, upper, k):
    product = jnp.einsum("rab,cbe->rcae", mult, upper, precision=lax.Precision.HIGHEST)
    below = rows_g > k
    trail = (below[:, None] & (cols_g > k)[None, :])[:, :, None, None]
    store = (below[:, None] & (cols_g == k)[None, :])[:, :, None, None]
    out = jnp.where(trail, blocks - product, blocks)
    return jnp.where(store, mult[:, None], out)


def drop_one(array, index, axis_pos):
    return jnp.concatenate(
        [
            lax.slice_in_dim(array, 0, index, axis=axis_pos),
            lax.slice_in_dim(array, index + 1, array.shape[axis_pos], axis=axis_pos),
        ],
        axis=axis_pos,
    )


def put_one(array, piece, index, axis_pos):
    return jnp.concatenate(
        [lax.slice_in_dim(array, 0, index, axis=axis_pos), piece, array], axis=axis_pos
    )


def factor_panel(column, row, k, shift, nprow, npcol):
    root_row, loc_row = (k % nprow, k // nprow)
    root_col = k % npcol
    column = spread(column, "pcol", root_col)
    inverse = spread_inverse(column[loc_row], shift, root_row)
    mult = jnp.einsum("rab,be->rae", column, inverse, precision=lax.Precision.HIGHEST)
    upper = broadcast_by_axis(row, PROW, root_row)
    return (mult, upper)


def body(values, pattern):
    rows_loc, cols_loc, width = (values.shape[0], values.shape[2], values.shape[4])
    nprow = lax.axis_size(PROW)
    npcol = lax.axis_size("pcol")
    rows_g = jnp.arange(rows_loc, dtype=jnp.int32) * nprow + lax.axis_index(PROW)
    cols_g = jnp.arange(cols_loc, dtype=jnp.int32) * npcol + lax.axis_index("pcol")
    shift = shift_coef * math.sqrt(width)
    eye = jnp.eye(width, dtype=jnp.float32)
    blocks = values[:, 0, :, 0] * pattern[:, 0, :, 0].astype(jnp.float32)[:, :, None, None]
    diag = jnp.where(rows_g[:, None] == cols_g[None, :], shift, 0.0).astype(jnp.float32)
    blocks = blocks + diag[:, :, None, None] * eye
    row_first, col_first = (0 // nprow, 0 // npcol)
    row_next, col_next = (1 // nprow, 1 // npcol)
    mult_first, upper_first = factor_panel(
        blocks[:, col_first], blocks[row_first], 0, shift, nprow, npcol
    )
    column = apply_panel(
        blocks[:, col_next : col_next + 1],
        rows_g,
        cols_g[col_next : col_next + 1],
        mult_first,
        upper_first[col_next : col_next + 1],
        0,
    )[:, 0]
    row = apply_panel(
        blocks[row_next : row_next + 1],
        rows_g[row_next : row_next + 1],
        cols_g,
        mult_first[row_next : row_next + 1],
        upper_first,
        0,
    )[0]
    mult_next, upper_next = factor_panel(column, row, 1, shift, nprow, npcol)
    inner = drop_one(drop_one(blocks, row_next, 0), col_next, 1)
    inner = apply_panel(
        inner,
        drop_one(rows_g, row_next, 0),
        drop_one(cols_g, col_next, 0),
        drop_one(mult_first, row_next, 0),
        drop_one(upper_first, col_next, 0),
        0,
    )
    inner = put_one(inner, drop_one(column, row_next, 0)[:, None], col_next, 1)
    blocks = put_one(inner, row[None], row_next, 0)
    blocks = apply_panel(blocks, rows_g, cols_g, mult_next, upper_next, 1)
    return blocks[:, None, :, None]


def solution(mesh):
    torus = Mesh(mesh.devices.reshape(2, 4, mesh.shape["pcol"]), ("prow_0", "prow_1", "pcol"))
    return jax.shard_map(
        body,
        mesh=torus,
        in_specs=(P(None, PROW, None, "pcol", None, None), P(None, PROW, None, "pcol")),
        out_specs=P(None, PROW, None, "pcol", None, None),
        check_vma=False,
    )
```

profile of v0, /device:TPU:49, one launch (start us, length us, event | category | flops | bytes accessed | tf_op | source)
XLA Modules:
  0.0 462.6 jit_solution(778879318605547930)
XLA Ops:
  7.4 0.7 convert_element_type.19
  8.1 0.1 compare_select_fusion
  8.2 12.2 %fusion.2 = f32[12,4,256,256]{3,2,0,1:T(8,128)} fusion(f32[12,1,4,1,256,256]{5,4,3,2,1,0:T(8,128)} %param.2, f32[256,256]{1,0:T(8,128)S(1)} %fusion.18, f32[12,4]{0,1:T(4,128)S(1)} %compare_select_fusion, f32[12,4]{0,1:T(4,128)S(1)} %bitcast.93), kind=kLoop, calls=%fused_computation.5 | loop fusion | flops 9437184 | bytes 25428352 | tf_op jit(solution)/shard_map/add | solution.py:102
  20.4 3.8 slice_select_fusion
  24.2 74.5 %reduce-scatter.3.cloned.1.call-done = f32[192,256]{1,0:T(8,128)} async-done(((f32[3072,256]{1,0:T(8,128)}), f32[192,256]{1,0:T(8,128)}) %reduce-scatter.3.cloned.1.call-update) | async-done | bytes 196624 | tf_op jit(solution)/shard_map/reduce_scatter | solution.py:32
  98.8 0.0 all-reduce.5.cloned.1.call-start
  98.9 2.3 select_bitcast_fusion.1
  101.2 65.2 %all-gather.7.cloned.1.call-done = f32[3072,256]{1,0:T(8,128)} async-done(((f32[192,256]{1,0:T(8,128)}), f32[3072,256]{1,0:T(8,128)}) %all-gather.7.cloned.1.call-update) | async-done | bytes 3145744 | tf_op jit(solution)/shard_map/all_gather | solution.py:33
  166.5 1.3 convolution_subtract_fusion.5
  167.8 0.4 fusion.12
  168.2 1.3 convolution_subtract_fusion.4
  169.5 0.4 fusion.42
  169.9 1.3 convolution_subtract_fusion.3
  171.2 1.1 fusion.43
  172.3 0.0 all-reduce.7.cloned.1.call-start
  172.4 0.5 all-reduce.7.cloned.1.call-update
  172.9 0.0 reduce-scatter.5.cloned.1.call-start
  173.1 40.2 %all-gather.11.cloned.1.call-done = f32[2048,256]{1,0:T(8,128)} async-done(((f32[256,256]{1,0:T(8,128)}), f32[2048,256]{1,0:T(8,128)}) %all-gather.11.cloned.1.call-update) | async-done | bytes 2097168 | tf_op jit(solution)/shard_map/all_gather | solution.py:17
  213.2 4.5 fusion.16
  217.8 10.0 %all-reduce.7.cloned.1.call-done = f32[4,256,256]{2,1,0:T(8,128)} async-done(((f32[4,256,256]{2,1,0:T(8,128)}), f32[4,256,256]{2,1,0:T(8,128)}) %all-reduce.7.cloned.1.call-update) | async-done | bytes 1048592 | tf_op jit(solution)/shard_map/psum | solution.py:39
  227.7 6.1 %broadcast_select_fusion = (f32[12,1,256,256]{3,2,0,1:T(8,128)}, f32[12,1,256,256]{3,2,0,1:T(8,128)}) fusion(pred[]{:T(512)S(6)} %eq.80, f32[12,256,256]{2,1,0:T(8,128)S(1)} %fusion.16, f32[4,256,256]{2,1,0:T(8,128)} %all-reduce.7.cloned.1.call-done, f32[12,4,256,256]{3,2,0,1:T(8,128)} %fusion.2, pred[12]{0:T(512)(128)(4,1)S(1)} %get-tuple-element.13, ...), kind=kOutput, calls=%fused_computation.13 | convolution fusion | flops 2419064832 | bytes 15991809 | tf_op jit(solution)/shard_map/rab,cbe->rcae/dot_general | solution.py:58
  233.9 75.9 %reduce-scatter.5.cloned.1.call-done = f32[192,256]{1,0:T(8,128)} async-done(((f32[3072,256]{1,0:T(8,128)}), f32[192,256]{1,0:T(8,128)}) %reduce-scatter.5.cloned.1.call-update) | async-done | bytes 196624 | tf_op jit(solution)/shard_map/reduce_scatter | solution.py:32
  309.9 0.0 all-reduce.9.cloned.1.call-start
  310.0 2.7 fusion.7
  312.7 1.1 copy-done.2
  313.8 1.1 select_bitcast_fusion
  314.9 0.2 all-gather.13.cloned.1.call-start
  315.2 48.3 %all-gather.9.cloned.1.call-done = f32[3072,256]{1,0:T(8,128)} async-done(((f32[192,256]{1,0:T(8,128)}), f32[3072,256]{1,0:T(8,128)}) %all-gather.9.cloned.1.call-update) | async-done | bytes 3145744 | tf_op jit(solution)/shard_map/all_gather | solution.py:33
  363.5 1.3 convolution_subtract_fusion.2
  364.8 0.4 fusion.9
  365.2 1.3 convolution_subtract_fusion.1
  366.5 0.4 fusion.44
  366.9 1.3 convolution_subtract_fusion
  368.3 1.1 fusion.45
  369.4 0.0 all-reduce.11.cloned.1.call-start
  369.5 0.1 slice_compare_fusion
  369.5 0.1 slice_compare_fusion.2
  369.6 0.1 broadcast_and_fusion.1
  369.7 0.1 broadcast_and_fusion.3
  369.8 1.5 copy-done.1
  371.3 1.9 slice.75
  373.3 0.9 slice-done
  374.2 12.7 %fusion.3 = f32[11,3,256,256]{3,2,0,1:T(8,128)} fusion(f32[12,4,256,256]{3,2,0,1:T(8,128)} %fusion.2, f32[11,256,256]{2,1,0:T(8,128)S(1)} %slice-done, pred[11,3]{0,1:T(4,128)(4,1)S(1)} %get-tuple-element.8, pred[11,3]{0,1:T(4,128)(4,1)S(1)} %get-tuple-element.7, f32[4,256,256]{2,1,0:T(8,128)} %all-reduce.7.cloned.1.call-done), kind=kOutput, calls=%fused_computation.6 | convolution fusion | flops 6650265600 | bytes 23856128 | tf_op jit(solution)/shard_map/rab,cbe->rcae/dot_general | solution.py:58
  386.9 23.5 %all-gather.13.cloned.1.call-done = f32[2048,256]{1,0:T(8,128)} async-done(((f32[256,256]{1,0:T(8,128)}), f32[2048,256]{1,0:T(8,128)}) %all-gather.13.cloned.1.call-update) | async-done | bytes 2097168 | tf_op jit(solution)/shard_map/all_gather | solution.py:17
  410.4 6.3 %fusion.15 = f32[12,256,256]{2,1,0:T(8,128)} fusion(f32[12,256,256]{2,1,0:T(8,128)} %bitcast.91, f32[2048,256]{1,0:T(8,128)} %all-gather.13.cloned.1.call-done), kind=kOutput, calls=%fused_computation.33 | convolution fusion | flops 2415919104 | bytes 6553600 | tf_op jit(solution)/shard_map/rab,be->rae/dot_general | solution.py:87
  416.7 9.3 %all-reduce.11.cloned.1.call-done = f32[4,256,256]{2,1,0:T(8,128)} async-done(((f32[4,256,256]{2,1,0:T(8,128)}), f32[4,256,256]{2,1,0:T(8,128)}) %all-reduce.11.cloned.1.call-update) | async-done | bytes 1048592 | tf_op jit(solution)/shard_map/psum | solution.py:39
  426.0 18.2 %fusion.1 = f32[12,1,4,1,256,256]{5,4,0,2,3,1:T(8,128)} fusion(f32[11,3,256,256]{3,2,0,1:T(8,128)} %fusion.3, f32[11,1,256,256]{3,2,0,1:T(8,128)} %slice.75, f32[1,4,256,256]{3,2,0,1:T(8,128)S(1)} %copy-done.3, f32[12,256,256]{2,1,0:T(8,128)} %fusion.15, pred[12,4]{0,1:T(4,128)(4,1)S(1)} %get-tuple-element.6, pred[12,4]{0,1:T(4,128)(4,1)S(1)} %get-tuple-element.5, ...), kind=kOutput, calls=%fused_computation.3 | convolution fusion | flops 9679405056 | bytes 29360224 | tf_op jit(solution)/shard_map/rab,cbe->rcae/dot_general | solution.py:58
  444.2 10.8 %copy.10 = f32[12,1,4,1,256,256]{5,4,3,2,1,0:T(8,128)} copy(f32[12,1,4,1,256,256]{5,4,0,2,3,1:T(8,128)} %fusion.1) | data formatting | bytes 25165824 | tf_op jit(solution)/shard_map/broadcast_in_dim | solution.py:137
  (30 shorter events, 0.4 us)
Async XLA Ops:
  7.4 91.4 %reduce-scatter.3.cloned.1.call-start = ((), (), s32[]{:S(2)}) async-start(), calls=%async_computation.2 | async-start | bytes 3342336 | tf_op jit(solution)/shard_map/reduce_scatter | solution.py:32
  24.2 142.3 %all-gather.7.cloned.1.call-start = ((), (), s32[]{:S(2)}) async-start(), calls=%async_computation.3 | async-start | bytes 3342336 | tf_op jit(solution)/shard_map/all_gather | solution.py:33
  98.8 73.6 %all-reduce.5.cloned.1.call-start = ((), (), s32[]{:S(2)}) async-start(), calls=%async_computation.4 | async-start | bytes 2097152 | tf_op jit(solution)/shard_map/psum | solution.py:39
  101.2 112.1 %all-gather.11.cloned.1.call-start = ((), (), s32[]{:S(2)}) async-start(), calls=%async_computation.10 | async-start | bytes 2359296 | tf_op jit(solution)/shard_map/all_gather | solution.py:17
  172.3 55.4 %all-reduce.7.cloned.1.call-start = ((), (), s32[]{:S(2)}) async-start(), calls=%async_computation.5 | async-start | bytes 2097152 | tf_op jit(solution)/shard_map/psum | solution.py:39
  172.9 136.9 %reduce-scatter.5.cloned.1.call-start = ((), (), s32[]{:S(2)}) async-start(), calls=%async_computation.6 | async-start | bytes 3342336 | tf_op jit(solution)/shard_map/reduce_scatter | solution.py:32
  217.8 152.0 %copy-start = (f32[12,256,256]{2,1,0:T(8,128)}, f32[12,256,256]{2,1,0:T(8,128)S(1)}, u32[]{:S(2)}) copy-start(f32[12,256,256]{2,1,0:T(8,128)S(1)} %fusion.16) | copy-start | bytes 9437188
  233.9 129.6 %all-gather.9.cloned.1.call-start = ((), (), s32[]{:S(2)}) async-start(), calls=%async_computation.7 | async-start | bytes 3342336 | tf_op jit(solution)/shard_map/all_gather | solution.py:33
  309.9 63.4 %all-reduce.9.cloned.1.call-start = ((), (), s32[]{:S(2)}) async-start(), calls=%async_computation.8 | async-start | bytes 2097152 | tf_op jit(solution)/shard_map/psum | solution.py:39
  312.7 1.1 copy-start.2
  314.9 95.4 %all-gather.13.cloned.1.call-start = ((), (), s32[]{:S(2)}) async-start(), calls=%async_computation.11 | async-start | bytes 2359296 | tf_op jit(solution)/shard_map/all_gather | solution.py:17
  369.4 56.6 %all-reduce.11.cloned.1.call-start = ((), (), s32[]{:S(2)}) async-start(), calls=%async_computation.9 | async-start | bytes 2097152 | tf_op jit(solution)/shard_map/psum | solution.py:39
  369.4 1.9 copy-start.1
  371.3 2.9 slice-start
  410.4 15.6 %copy-start.3 = (f32[1,4,256,256]{3,2,0,1:T(8,128)S(1)}, f32[1,4,256,256]{3,2,0,1:T(8,128)}, u32[]{:S(2)}) copy-start(f32[1,4,256,256]{3,2,0,1:T(8,128)} %copy-done.2) | copy-start | bytes 3145732
Sparse Core Ops, SparseCore 0:
  24.3 74.4 reduce-scatter.2
  101.2 65.1 all-gather.6
  172.5 40.7 all-gather.10
  234.0 75.8 reduce-scatter.4
  312.2 51.2 all-gather.8
  369.5 40.8 all-gather.12
Sparse Core Ops, SparseCore 1:
  101.7 48.2 all-reduce.4
  175.3 52.4 all-reduce.6
  315.0 51.8 all-reduce.8
  373.4 52.6 all-reduce.10
where the time goes:
time: 467 us; the launch traced here: 463 us
  waiting for transfers between devices  348 us (75%)
  matrix products  62.1 us (13%)
  other arithmetic  20.5 us (4%)
  local copies, waits for them, and re-layouts  16.2 us (3%)
  between operations  15.4 us (3%)
    reduce_scatter x2, waiting for transfers between devices, spread(): own = lax.psum_scatter(padded, axis, scatter_dimension=0, tiled=True)  150 us
    all_gather x2, waiting for transfers between devices, spread(): lax.all_gather(own, axis, axis=0, tiled=True)[:len(lines)]  114 us
    all_gather x2, waiting for transfers between devices, picked(): lax.all_gather(value, axis)  63.7 us
    dot_general x4, matrix products, apply_panel(): jnp.einsum('rab,cbe->rcae', mult, upper, precision=lax.Precision.HIGHEST)  39.7 us
    psum x4, waiting for transfers between devices, broadcast_by_axis(): value = lax.psum(value, axis)  19.3 us
    add x1, other arithmetic, body(): blocks = blocks + diag[:, :, None, None] * eye  12.2 us
    dot_general x2, matrix products, factor_panel(): jnp.einsum('rab,be->rae', column, inverse, precision=lax.Precision.HIGHEST)  10.8 us
    broadcast_in_dim x1, local copies, waits for them, and re-layouts, body(): return blocks[:, None, :, None]  10.8 us
  transfers between devices with their start and end apart: 10, of which 8 were waited for; matrix products, arithmetic and copies ran while one was open for 9% of the time, Pallas kernels for 0%

commit v1 on v0

v1 whole, which is shorter than its diff:
```python
import functools
import math

import jax
import jax.numpy as jnp
from jax import lax
from jax.experimental import pallas as pl
from jax.experimental.pallas import tpu as pltpu
from jax.sharding import PartitionSpec as P

SWEEPS = 3
SHIFT_COEF = 5.0
MESH = pl.DeviceIdType.MESH

TREES = (
    ((0, 0, 1, 0), (1, 0, 2, 0), (1, 0, 1, 1), (2, 0, 3, 0), (1, 1, 2, 1), (1, 1, 0, 1), (2, 1, 3, 1)),
    ((0, 0, 3, 0), (3, 0, 2, 0), (3, 0, 3, 1), (2, 0, 1, 0), (3, 1, 2, 1), (3, 1, 0, 1), (2, 1, 1, 1)),
    ((0, 0, 1, 0), (1, 0, 2, 0), (2, 0, 3, 0), (2, 0, 2, 1), (2, 1, 3, 1), (2, 1, 1, 1), (3, 1, 0, 1)),
    ((0, 0, 3, 0), (0, 0, 0, 1), (3, 0, 2, 0), (0, 1, 1, 1), (0, 1, 3, 1), (2, 0, 1, 0), (1, 1, 2, 1)),
)
NT = len(TREES)


def tree_depths(edges):
    depth = {(0, 0): 0}
    for a, b, c, d in edges:
        depth[c, d] = depth[a, b] + 1
    return depth


DEPTHS = tuple(tree_depths(edges) for edges in TREES)
MAX_DEPTH = max(max(d.values()) for d in DEPTHS)


def lookup(node, table):
    out = jnp.int32(0)
    for (a, b), value in table.items():
        if value:
            out = jnp.where(node == a * 2 + b, jnp.int32(value), out)
    return out


def split(x):
    high = x.astype(jnp.bfloat16)
    return high, (x - high.astype(jnp.float32)).astype(jnp.bfloat16)


def dot(a, b):
    return jnp.dot(a, b, preferred_element_type=jnp.float32)


def mm(a, b):
    ah, al = split(a)
    bh, bl = split(b)
    return dot(ah, bh) + (dot(ah, bl) + dot(al, bh))


def eye_of(width):
    rows = lax.broadcasted_iota(jnp.int32, (width, width), 0)
    cols = lax.broadcasted_iota(jnp.int32, (width, width), 1)
    return jnp.where(rows == cols, 1.0, 0.0).astype(jnp.float32)


def comm_kernel(
    dims, pat, values, cols_out, vh_out, vl_out, fix_out,
    colbuf, rowbuf, piv, vtmp, xs,
    load_sem, col_send, col_recv, row_send, row_recv, piv_send, piv_recv,
    sib_send, sib_recv, sibp_send, sibp_recv, out_sem,
):
    nr, nc, width, shift = dims
    qr = width // NT
    p = lax.axis_index("prow")
    q = lax.axis_index("pcol")
    xlo, z = p // 4, p % 4
    y, xhi, core = q // 4, (q // 2) % 2, q % 2
    other = 1 - core

    def dev(xlo_, z_, y_, xhi_, core_):
        return (xlo_ * 4 + z_, y_ * 4 + xhi_ * 2 + core_)

    sibling = dev(xlo, z, y, xhi, other)
    barrier = pltpu.get_barrier_semaphore()
    partners = (
        sibling,
        dev(xlo, z, (y + 1) % 4, xhi, core),
        dev(xlo, z, (y + 3) % 4, xhi, core),
        dev(xlo, z, y, 1 - xhi, core),
        dev(xlo, (z + 1) % 4, y, xhi, core),
        dev(xlo, (z + 3) % 4, y, xhi, core),
        dev(1 - xlo, z, y, xhi, core),
    )
    for partner in partners:
        pl.semaphore_signal(barrier, inc=1, device_id=partner, device_id_type=MESH)

    cnode = y * 2 + xhi
    cdepth = [lookup(cnode, d) for d in DEPTHS]
    rnode = [((z + 4 - k) % 4) * 2 + xlo for k in range(2)]
    rdepth = [[lookup(rnode[k], d) for d in DEPTHS] for k in range(2)]
    cmax = cdepth[0]
    for d in cdepth[1:]:
        cmax = jnp.maximum(cmax, d)

    def children(tree, node, place):
        kids = {}
        for a, b, c, d in TREES[tree]:
            kids.setdefault((a, b), []).append((c, d))
        out = []
        for slot in range(max(len(v) for v in kids.values())):
            has = {n: 1 for n, v in kids.items() if len(v) > slot}
            to_a = lookup(node, {n: v[slot][0] for n, v in kids.items() if len(v) > slot})
            to_b = lookup(node, {n: v[slot][1] for n, v in kids.items() if len(v) > slot})
            out.append((lookup(node, has) == 1, place(to_a, to_b)))
        return out

    ckids = [children(t, cnode, lambda a, b: dev(xlo, z, a, b, core)) for t in range(NT)]
    rkids = [
        [children(t, rnode[k], lambda a, b, k=k: dev(b, (a + k) % 4, y, xhi, core)) for t in range(NT)]
        for k in range(2)
    ]

    def remote(src, dst, send, recv, device):
        return pltpu.make_async_remote_copy(
            src_ref=src, dst_ref=dst, send_sem=send, recv_sem=recv,
            device_id=device, device_id_type=MESH,
        )

    def send_col(t, u):
        ref = colbuf.at[core, u, pl.ds(t * qr, qr)]
        for slot, (has, device) in enumerate(ckids[t]):
            pl.when(has)(remote(ref, ref, col_send.at[t, slot], col_recv.at[t, u], device).start)

    def send_row(k, t, v):
        ref = rowbuf.at[k, v, pl.ds(t * qr, qr)]
        for slot, (has, device) in enumerate(rkids[k][t]):
            pl.when(has)(remote(ref, ref, row_send.at[k, t, slot], row_recv.at[k, t, v], device).start)

    def send_piv(k, t):
        ref = piv.at[k, core, pl.ds(t * qr, qr)]
        for slot, (has, device) in enumerate(rkids[k][t]):
            pl.when(has)(remote(ref, ref, piv_send.at[k, t, slot], piv_recv.at[k, t], device).start)
        remote(ref, ref, sibp_send.at[k], sibp_recv.at[k, t], sibling).start()

    def sib_copy(u):
        ref = colbuf.at[core, u]
        return remote(ref, ref, sib_send, sib_recv.at[u], sibling)

    def arrive(ref, sem):
        pltpu.make_async_copy(ref, ref, sem).wait()

    eye = eye_of(width)
    col_root = cnode == 0
    row_root = [p == k for k in range(2)]

    @pl.when(col_root)
    def _():
        for u in range(nr):
            pltpu.make_async_copy(values.at[u, 0], colbuf.at[core, u], load_sem.at[u]).start()

    for k in range(2):
        @pl.when(row_root[k])
        def _():
            for v in range(nc):
                pltpu.make_async_copy(values.at[0, v], rowbuf.at[k, v], load_sem.at[nr + v]).start()

    pl.semaphore_wait(barrier, len(partners))

    for k in range(2):
        @pl.when(row_root[k])
        def _():
            for v in range(nc):
                pltpu.make_async_copy(values.at[0, v], rowbuf.at[k, v], load_sem.at[nr + v]).wait()
                block = rowbuf[k, v] * pat[v].astype(jnp.float32)
                if v == 0:
                    block = block + jnp.where(q == k, shift, 0.0).astype(jnp.float32) * eye
                rowbuf[k, v] = block

    def own_piv(k, t):
        piv[k, core, pl.ds(t * qr, qr)] = colbuf[core, 0, pl.ds(t * qr, qr)]
        send_piv(k, t)

    @pl.when(col_root)
    def _():
        def one(u, carry):
            pltpu.make_async_copy(values.at[u, 0], colbuf.at[core, u], load_sem.at[u]).wait()
            on_diag = (u == 0) & (p == core)
            block = colbuf[core, u] * pat[u * nc].astype(jnp.float32)
            colbuf[core, u] = block + jnp.where(on_diag, shift, 0.0).astype(jnp.float32) * eye
            for t in range(NT):
                send_col(t, u)
            sib_copy(u).start()
            return carry

        one(0, 0)
        for k in range(2):
            @pl.when(row_root[k])
            def _():
                for t in range(NT):
                    own_piv(k, t)
        lax.fori_loop(1, nr, one, 0)

    for k in range(2):
        @pl.when(row_root[k])
        def _():
            for v in range(nc):
                for t in range(NT):
                    send_row(k, t, v)

    def relay(s):
        for t in range(NT):
            u = s - cdepth[t]

            @pl.when((cdepth[t] > 0) & (u >= 0) & (u < nr))
            def _():
                arrive(colbuf.at[core, u, pl.ds(t * qr, qr)], col_recv.at[t, u])
                send_col(t, u)

                for k in range(2):
                    @pl.when(row_root[k] & (u == 0))
                    def _():
                        own_piv(k, t)

        for k in range(2):
            for t in range(NT):
                @pl.when((rdepth[k][t] > 0) & (s == cdepth[t] + rdepth[k][t]))
                def _():
                    arrive(piv.at[k, core, pl.ds(t * qr, qr)], piv_recv.at[k, t])
                    send_piv(k, t)

        for k in range(2):
            for t in range(NT):
                w = s - rdepth[k][t]

                @pl.when((rdepth[k][t] > 0) & (w >= 0) & (w < 2 * nc) & (w % 2 == 0))
                def _():
                    v = w // 2
                    arrive(rowbuf.at[k, v, pl.ds(t * qr, qr)], row_recv.at[k, t, v])
                    send_row(k, t, v)

        done = s - cmax

        @pl.when((cmax > 0) & (done >= 0) & (done < nr))
        def _():
            sib_copy(done).start()

    def newton_steps(block_ref, out):
        def first():
            block = block_ref[...]
            xs[out] = (2.0 * eye - block * (1.0 / shift)) * (1.0 / shift)

        def inner():
            xs[4] = 2.0 * eye - mm(block_ref[...], xs[out])

        def outer():
            xs[out] = mm(xs[out], xs[4])

        steps = [first]
        for _ in range(SWEEPS - 1):
            steps += [inner, outer]
        return steps

    def wait_piv():
        for k in range(2):
            for t in range(NT):
                ref = piv.at[k, other, pl.ds(t * qr, qr)]
                arrive(ref, sibp_recv.at[k, t])

    def middle():
        xs[2] = mm(piv[1, 0], xs[0])

    def schur():
        xs[3] = piv[1, 1] - mm(xs[2], piv[0, 1])

    def u_one():
        for c in range(nc):
            vtmp[1, c] = rowbuf[1, c] - mm(xs[2], rowbuf[0, c])

        @pl.when(p == 1)
        def _():
            fix_out[...] = vtmp[1]

            @pl.when(q == 0)
            def _():
                fix_out[0] = xs[2]

        @pl.when(q < 2)
        def _():
            vtmp[1, 0] = jnp.where(q == 1, -1.0, 0.0).astype(jnp.float32) * eye

    def put_v(k, c, value):
        high, low = split(value)
        vh_out[c, pl.ds(k * width, width)] = high
        vl_out[c, pl.ds(k * width, width)] = low

    def v_one():
        for c in range(nc):
            value = mm(xs[1], vtmp[1, c])
            vtmp[1, c] = value
            put_v(1, c, value)

    def v_mid():
        for c in range(nc):
            upper = rowbuf[0, c]
            if c == 0:
                upper = jnp.where(q < 2, jnp.where(q == 0, -1.0, 0.0).astype(jnp.float32) * eye, upper)
            vtmp[0, c] = upper - mm(piv[0, 1], vtmp[1, c])

    def v_zero():
        for c in range(nc):
            put_v(0, c, mm(xs[0], vtmp[0, c]))

    work = [wait_piv]
    work += newton_steps(piv.at[0, 0], 0)
    work += [middle, schur]
    work += newton_steps(xs.at[3], 1)
    tail = [u_one, v_one, v_mid, v_zero]
    first_step = 2 * MAX_DEPTH + 1
    last = max(nr, 2 * nc) + MAX_DEPTH
    slots = max(last - first_step, 1)
    per = -(-len(work) // slots)

    def step(s, carry):
        relay(s)
        for i in range(slots):
            part = work[i * per:(i + 1) * per]
            if part:
                @pl.when(s == first_step + i)
                def _():
                    for item in part:
                        item()
        return carry

    lax.fori_loop(0, last, step, 0)

    def out_copy(k, u):
        return pltpu.make_async_copy(colbuf.at[k, u], cols_out.at[k, u], out_sem)

    for u in range(nr):
        arrive(colbuf.at[other, u], sib_recv.at[u])
    whole = pltpu.make_async_copy(colbuf, cols_out, out_sem)
    whole.start()
    for item in tail:
        item()

    for t in range(NT):
        for slot, (has, _) in enumerate(ckids[t]):
            ref = colbuf.at[0, pl.ds(0, nr), pl.ds(0, qr)]
            pl.when(has)(functools.partial(arrive, ref, col_send.at[t, slot]))
        for k in range(2):
            for slot, (has, _) in enumerate(rkids[k][t]):
                ref = rowbuf.at[0, pl.ds(0, nc), pl.ds(0, qr)]
                pl.when(has)(functools.partial(arrive, ref, row_send.at[k, t, slot]))
                ref = piv.at[0, 0, pl.ds(0, qr)]
                pl.when(has)(functools.partial(arrive, ref, piv_send.at[k, t, slot]))
    arrive(colbuf.at[core], sib_send)
    for k in range(2):
        arrive(piv.at[0, 0], sibp_send.at[k])
    whole.wait()


def update_kernel(dims, pat, values, cols, vh, vl, fix, out):
    nr, nc, width, shift = dims
    r = pl.program_id(0)
    p = lax.axis_index("prow")
    q = lax.axis_index("pcol")
    row = r * 8 + p
    eye = eye_of(width)

    def base(c):
        on_diag = row == c * 16 + q
        block = values[0, c] * pat[r * nc + c].astype(jnp.float32)
        return block + jnp.where(on_diag, shift, 0.0).astype(jnp.float32) * eye

    @pl.when(row == 0)
    def _():
        for c in range(nc):
            out[0, c] = base(c)

    @pl.when(row == 1)
    def _():
        out[0] = fix[...]

    @pl.when(row > 1)
    def _():
        c0h, c0l = split(cols[0, 0])
        c1h, c1l = split(cols[1, 0])
        high = jnp.concatenate([c0h, c1h], axis=1)
        low = jnp.concatenate([c0l, c1l], axis=1)
        for c in range(nc):
            prod = dot(high, vh[c]) + (dot(high, vl[c]) + dot(low, vh[c]))
            keep = base(c)
            if c == 0:
                keep = jnp.where(q < 2, 0.0, 1.0).astype(jnp.float32) * keep
            out[0, c] = keep - prod


def body(values, pattern):
    nr, _, nc, _, width, _ = values.shape
    shift = SHIFT_COEF * math.sqrt(width)
    dims = (nr, nc, width, shift)
    vals = values.reshape(nr, nc, width, width)
    pat = pattern.reshape(nr * nc)
    f32, bf16 = jnp.float32, jnp.bfloat16
    vmem = pl.BlockSpec(memory_space=pltpu.VMEM)
    dma = pltpu.SemaphoreType.DMA
    cols, vh, vl, fix = pl.pallas_call(
        functools.partial(comm_kernel, dims),
        out_shape=(
            jax.ShapeDtypeStruct((2, nr, width, width), f32),
            jax.ShapeDtypeStruct((nc, 2 * width, width), bf16),
            jax.ShapeDtypeStruct((nc, 2 * width, width), bf16),
            jax.ShapeDtypeStruct((nc, width, width), f32),
        ),
        in_specs=[pl.BlockSpec(memory_space=pltpu.SMEM), pl.BlockSpec(memory_space=pl.ANY)],
        out_specs=(pl.BlockSpec(memory_space=pl.ANY), vmem, vmem, vmem),
        scratch_shapes=[
            pltpu.VMEM((2, nr, width, width), f32),
            pltpu.VMEM((2, nc, width, width), f32),
            pltpu.VMEM((2, 2, width, width), f32),
            pltpu.VMEM((2, nc, width, width), f32),
            pltpu.VMEM((5, width, width), f32),
            dma((nr + nc,)),
            dma((NT, 2)),
            dma((NT, nr)),
            dma((2, NT, 2)),
            dma((2, NT, nc)),
            dma((2, NT, 2)),
            dma((2, NT)),
            dma,
            dma((nr,)),
            dma((2,)),
            dma((2, NT)),
            dma,
        ],
        compiler_params=pltpu.CompilerParams(
            collective_id=0, has_side_effects=True, vmem_limit_bytes=40 << 20
        ),
        name="gather_panels",
    )(pat, vals)
    whole = lambda *shape: pl.BlockSpec(shape, lambda r: (0,) * len(shape))
    out = pl.pallas_call(
        functools.partial(update_kernel, dims),
        grid=(nr,),
        out_shape=jax.ShapeDtypeStruct((nr, nc, width, width), f32),
        in_specs=[
            pl.BlockSpec(memory_space=pltpu.SMEM),
            pl.BlockSpec((1, nc, width, width), lambda r: (r, 0, 0, 0)),
            pl.BlockSpec((2, 1, width, width), lambda r: (0, r, 0, 0)),
            whole(nc, 2 * width, width),
            whole(nc, 2 * width, width),
            whole(nc, width, width),
        ],
        out_specs=pl.BlockSpec((1, nc, width, width), lambda r: (r, 0, 0, 0)),
        compiler_params=pltpu.CompilerParams(vmem_limit_bytes=40 << 20),
        cost_estimate=pl.CostEstimate(flops=6 * nr * nc * width**3 * 2, bytes_accessed=35 << 20, transcendentals=0),
        name="update_blocks",
    )(pat, vals, cols, vh, vl, fix)
    return out.reshape(values.shape)


def solution(mesh):
    return jax.shard_map(
        body,
        mesh=mesh,
        in_specs=(P(None, "prow", None, "pcol", None, None), P(None, "prow", None, "pcol")),
        out_specs=P(None, "prow", None, "pcol", None, None),
        check_vma=False,
    )
```

time: 467 us -> 101 us (0.22)
  the two profiles are of different devices: /device:TPU:49 before, /device:TPU:7 now
where the time goes in v1:
time: 101 us; the launch traced here: 100 us
  Pallas kernels  99.6 us (99%)
    pallas_call x1, Pallas kernels, body(): pl.pallas_call(functools.partial(comm_kernel, dims), out_shape=(jax.Shape...  81.6 us
    pallas_call x1, Pallas kernels, body(): pl.pallas_call(functools.partial(update_kernel, dims), grid=(nr,), out_sh...  18 us

profile of v1, /device:TPU:7, one launch (start us, length us, event | category | flops | bytes accessed | tf_op | source)
XLA Modules:
  0.0 100.4 jit_solution(12739119252975773382)
XLA Ops:
  0.0 0.8 copy.5
  0.8 0.1 reshape.9.pat
  0.9 81.6 %gather_panels.1 = (f32[2,12,256,256]{3,2,1,0:T(8,128)S(1)}, bf16[4,512,256]{2,1,0:T(8,128)(2,1)S(1)}, bf16[4,512,256]{2,1,0:T(8,128)(2,1)S(1)}, f32[4,256,256]{2,1,0:T(8,128)S(1)}) custom-call(s32[48]{0:T(128)S(1)} %reshape.9.pat, f32[12,4,256,256]{3,2,1,0:T(8,128)} %bitcast.6), custom_call_target="tpu_custom_call" | custom-call | tf_op jit(solution)/shard_map/gather_panels/pallas_call | solution.py:405
  82.4 18.0 %update_blocks.1 = f32[12,4,256,256]{3,2,1,0:T(8,128)} custom-call(s32[48]{0:T(128)S(1)} %reshape.9.pat, f32[12,4,256,256]{3,2,1,0:T(8,128)} %bitcast.7, f32[2,12,256,256]{3,2,1,0:T(8,128)S(1)} %get-tuple-element.9.cols, bf16[4,512,256]{2,1,0:T(8,128)(2,1)S(1)} %get-tuple-element.10.vh, bf16[4,512,256]{2,1,0:T(8,128)(2,1)S(1)} %get-tuple-element.11.vl, ...), custom_call_target="tpu_custom_call" | custom-call | flops 9663676416 | bytes 36700160 | tf_op jit(solution)/shard_map/update_blocks/pallas_call | solution.py:440

commit v2 on v1

--- a/solution.py
+++ b/solution.py
@@ -12,6 +12,12 @@
 SHIFT_COEF = 5.0
 MESH = pl.DeviceIdType.MESH
 
+COL_TREES = (
+    ((0, 0, 1, 0), (1, 0, 2, 0), (1, 0, 1, 1), (2, 0, 3, 0), (2, 0, 2, 1), (1, 1, 0, 1), (2, 1, 3, 1)),
+    ((0, 0, 3, 0), (3, 0, 2, 0), (3, 0, 3, 1), (2, 0, 1, 0), (3, 1, 2, 1), (3, 1, 0, 1), (2, 1, 1, 1)),
+    ((0, 0, 0, 1), (0, 1, 1, 1), (0, 1, 3, 1), (1, 1, 2, 1), (1, 1, 1, 0), (3, 1, 3, 0), (2, 1, 2, 0)),
+)
+NC_TREES = len(COL_TREES)
 TREES = (
     ((0, 0, 1, 0), (1, 0, 2, 0), (1, 0, 1, 1), (2, 0, 3, 0), (1, 1, 2, 1), (1, 1, 0, 1), (2, 1, 3, 1)),
     ((0, 0, 3, 0), (3, 0, 2, 0), (3, 0, 3, 1), (2, 0, 1, 0), (3, 1, 2, 1), (3, 1, 0, 1), (2, 1, 1, 1)),
@@ -19,6 +25,12 @@
     ((0, 0, 3, 0), (0, 0, 0, 1), (3, 0, 2, 0), (0, 1, 1, 1), (0, 1, 3, 1), (2, 0, 1, 0), (1, 1, 2, 1)),
 )
 NT = len(TREES)
+HOP = 3
+ROW_STEP = 4
+ROW_BASE = 4
+PIV_BASE = 13
+PACE = 4
+SLOTS = 3
 
 
 def tree_depths(edges):
@@ -28,8 +40,10 @@
     return depth
 
 
+COL_DEPTHS = tuple(tree_depths(edges) for edges in COL_TREES)
 DEPTHS = tuple(tree_depths(edges) for edges in TREES)
-MAX_DEPTH = max(max(d.values()) for d in DEPTHS)
+COL_DEPTH = max(max(d.values()) for d in COL_DEPTHS)
+ROW_DEPTH = max(max(d.values()) for d in DEPTHS)
 
 
 def lookup(node, table):
@@ -62,10 +76,10 @@
 
 
 def comm_kernel(
-    dims, pat, values, cols_out, vh_out, vl_out, fix_out,
-    colbuf, rowbuf, piv, vtmp, xs,
-    load_sem, col_send, col_recv, row_send, row_recv, piv_send, piv_recv,
-    sib_send, sib_recv, sibp_send, sibp_recv, out_sem,
+    dims, pat, values, colbuf, own, vh_out, vl_out, fix_out, flags,
+    rowbuf, piv, vtmp, xs,
+    own_sem, load_sem, root_sem, col_send, col_recv, row_send, row_recv, piv_send, piv_recv,
+    sib_send, sib_recv, sibp_send, sibp_recv,
 ):
     nr, nc, width, shift = dims
     qr = width // NT
@@ -93,16 +107,14 @@
         pl.semaphore_signal(barrier, inc=1, device_id=partner, device_id_type=MESH)
 
     cnode = y * 2 + xhi
-    cdepth = [lookup(cnode, d) for d in DEPTHS]
+    cdepth = [lookup(cnode, d) for d in COL_DEPTHS]
     rnode = [((z + 4 - k) % 4) * 2 + xlo for k in range(2)]
     rdepth = [[lookup(rnode[k], d) for d in DEPTHS] for k in range(2)]
-    cmax = cdepth[0]
-    for d in cdepth[1:]:
-        cmax = jnp.maximum(cmax, d)
-
-    def children(tree, node, place):
+    chunks = nr * NT // NC_TREES
+
+    def children(edges, node, place):
         kids = {}
-        for a, b, c, d in TREES[tree]:
+        for a, b, c, d in edges:
             kids.setdefault((a, b), []).append((c, d))
         out = []
         for slot in range(max(len(v) for v in kids.values())):
@@ -112,9 +124,9 @@
             out.append((lookup(node, has) == 1, place(to_a, to_b)))
         return out
 
-    ckids = [children(t, cnode, lambda a, b: dev(xlo, z, a, b, core)) for t in range(NT)]
+    ckids = [children(e, cnode, lambda a, b: dev(xlo, z, a, b, core)) for e in COL_TREES]
     rkids = [
-        [children(t, rnode[k], lambda a, b, k=k: dev(b, (a + k) % 4, y, xhi, core)) for t in range(NT)]
+        [children(e, rnode[k], lambda a, b, k=k: dev(b, (a + k) % 4, y, xhi, core)) for e in TREES]
         for k in range(2)
     ]
 
@@ -124,10 +136,13 @@
             device_id=device, device_id_type=MESH,
         )
 
-    def send_col(t, u):
-        ref = colbuf.at[core, u, pl.ds(t * qr, qr)]
+    def col_chunk(t, n):
+        return colbuf.at[core, NC_TREES * (n // NT) + t, pl.ds((n % NT) * qr, qr)]
+
+    def send_col(t, n):
+        ref = col_chunk(t, n)
         for slot, (has, device) in enumerate(ckids[t]):
-            pl.when(has)(remote(ref, ref, col_send.at[t, slot], col_recv.at[t, u], device).start)
+            pl.when(has)(remote(ref, ref, col_send.at[t, slot], col_recv.at[t, n], device).start)
 
     def send_row(k, t, v):
         ref = rowbuf.at[k, v, pl.ds(t * qr, qr)]
@@ -161,6 +176,9 @@
         def _():
             for v in range(nc):
                 pltpu.make_async_copy(values.at[0, v], rowbuf.at[k, v], load_sem.at[nr + v]).start()
+
+    for u in range(nr):
+        pltpu.make_async_copy(values.at[u], own.at[u], own_sem.at[u]).start()
 
     pl.semaphore_wait(barrier, len(partners))
 
@@ -178,69 +196,80 @@
         piv[k, core, pl.ds(t * qr, qr)] = colbuf[core, 0, pl.ds(t * qr, qr)]
         send_piv(k, t)
 
-    @pl.when(col_root)
-    def _():
-        def one(u, carry):
-            pltpu.make_async_copy(values.at[u, 0], colbuf.at[core, u], load_sem.at[u]).wait()
-            on_diag = (u == 0) & (p == core)
-            block = colbuf[core, u] * pat[u * nc].astype(jnp.float32)
-            colbuf[core, u] = block + jnp.where(on_diag, shift, 0.0).astype(jnp.float32) * eye
-            for t in range(NT):
-                send_col(t, u)
-            sib_copy(u).start()
-            return carry
-
-        one(0, 0)
-        for k in range(2):
-            @pl.when(row_root[k])
-            def _():
-                for t in range(NT):
-                    own_piv(k, t)
-        lax.fori_loop(1, nr, one, 0)
+    def one(u):
+        pltpu.make_async_copy(values.at[u, 0], colbuf.at[core, u], load_sem.at[u]).wait()
+        on_diag = (u == 0) & (p == core)
+        block = colbuf[core, u] * pat[u * nc].astype(jnp.float32)
+        colbuf[core, u] = block + jnp.where(on_diag, shift, 0.0).astype(jnp.float32) * eye
 
     for k in range(2):
         @pl.when(row_root[k])
         def _():
-            for v in range(nc):
+            for v in range(nc // 2):
                 for t in range(NT):
                     send_row(k, t, v)
 
+    def root_send(t, n):
+        ref = col_chunk(t, n)
+        return remote(ref, ref, root_sem.at[t, n], col_recv.at[t, n], ckids[t][0][1])
+
     def relay(s):
-        for t in range(NT):
-            u = s - cdepth[t]
-
-            @pl.when((cdepth[t] > 0) & (u >= 0) & (u < nr))
+        for k in range(2):
+            @pl.when(row_root[k] & (s == ROW_STEP))
             def _():
-                arrive(colbuf.at[core, u, pl.ds(t * qr, qr)], col_recv.at[t, u])
-                send_col(t, u)
-
-                for k in range(2):
-                    @pl.when(row_root[k] & (u == 0))
+                for v in range(nc // 2, nc):
+                    for t in range(NT):
+                        send_row(k, t, v)
+
+        for t in range(NC_TREES):
+            n = s - HOP * cdepth[t]
+
+            @pl.when((n >= 0) & (n < chunks))
+            def _():
+                @pl.when(cdepth[t] > 0)
+                def _():
+                    arrive(col_chunk(t, n), col_recv.at[t, n])
+                    send_col(t, n)
+
+                @pl.when(cdepth[t] == 0)
+                def _():
+                    @pl.when(n % NT == 0)
                     def _():
-                        own_piv(k, t)
+                        one(NC_TREES * (n // NT) + t)
+
+                    @pl.when(n >= PACE)
+                    def _():
+                        root_send(t, n - PACE).wait_send()
+
+                    root_send(t, n).start()
+
+                @pl.when(n % NT == NT - 1)
+                def _():
+                    sib_copy(NC_TREES * (n // NT) + t).start()
+
+                if t == 0:
+                    for i in range(NT):
+                        for k in range(2):
+                            @pl.when(row_root[k] & (n == i))
+                            def _():
+                                own_piv(k, i)
 
         for k in range(2):
             for t in range(NT):
-                @pl.when((rdepth[k][t] > 0) & (s == cdepth[t] + rdepth[k][t]))
+                @pl.when((rdepth[k][t] > 0) & (s == PIV_BASE + HOP * rdepth[k][t]))
                 def _():
                     arrive(piv.at[k, core, pl.ds(t * qr, qr)], piv_recv.at[k, t])
                     send_piv(k, t)
 
         for k in range(2):
             for t in range(NT):
-                w = s - rdepth[k][t]
-
-                @pl.when((rdepth[k][t] > 0) & (w >= 0) & (w < 2 * nc) & (w % 2 == 0))
+                w = s - ROW_BASE - HOP * rdepth[k][t]
+
+                @pl.when((rdepth[k][t] > 0) & (w >= 0) & (w < ROW_STEP * nc) & (w % ROW_STEP == 0))
                 def _():
-                    v = w // 2
+                    v = w // ROW_STEP
                     arrive(rowbuf.at[k, v, pl.ds(t * qr, qr)], row_recv.at[k, t, v])
                     send_row(k, t, v)
-
-        done = s - cmax
-
-        @pl.when((cmax > 0) & (done >= 0) & (done < nr))
-        def _():
-            sib_copy(done).start()
 
     def newton_steps(block_ref, out):
         def first():
@@ -313,8 +342,8 @@
     work += [middle, schur]
     work += newton_steps(xs.at[3], 1)
     tail = [u_one, v_one, v_mid, v_zero]
-    first_step = 2 * MAX_DEPTH + 1
-    last = max(nr, 2 * nc) + MAX_DEPTH
+    first_step = PIV_BASE + HOP * ROW_DEPTH + 1
+    last = max(chunks + HOP * COL_DEPTH, ROW_BASE + ROW_STEP * (nc - 1) + HOP * ROW_DEPTH + 1)
     slots = max(last - first_step, 1)
     per = -(-len(work) // slots)
 
@@ -331,20 +360,30 @@
 
     lax.fori_loop(0, last, step, 0)
 
-    def out_copy(k, u):
-        return pltpu.make_async_copy(colbuf.at[k, u], cols_out.at[k, u], out_sem)
-
     for u in range(nr):
         arrive(colbuf.at[other, u], sib_recv.at[u])
-    whole = pltpu.make_async_copy(colbuf, cols_out, out_sem)
-    whole.start()
     for item in tail:
         item()
 
+    def mark(u, carry):
+        for k in range(2):
+            flags[k * nr + u] = jnp.max(jnp.abs(colbuf[k, u]))
+        return carry
+
+    lax.fori_loop(0, nr, mark, 0)
+    for u in range(nr):
+        pltpu.make_async_copy(values.at[u], own.at[u], own_sem.at[u]).wait()
+
+    for t in range(NC_TREES):
+        for slot, (has, _) in enumerate(ckids[t]):
+            ref = colbuf.at[0, pl.ds(0, nr // NC_TREES)]
+            pl.when(has & (cnode > 0))(functools.partial(arrive, ref, col_send.at[t, slot]))
+
+        @pl.when(col_root)
+        def _():
+            for n in range(chunks - PACE, chunks):
+                root_send(t, n).wait_send()
     for t in range(NT):
-        for slot, (has, _) in enumerate(ckids[t]):
-            ref = colbuf.at[0, pl.ds(0, nr), pl.ds(0, qr)]
-            pl.when(has)(functools.partial(arrive, ref, col_send.at[t, slot]))
         for k in range(2):
             for slot, (has, _) in enumerate(rkids[k][t]):
                 ref = rowbuf.at[0, pl.ds(0, nc), pl.ds(0, qr)]
@@ -354,43 +393,69 @@
     arrive(colbuf.at[core], sib_send)
     for k in range(2):
         arrive(piv.at[0, 0], sibp_send.at[k])
-    whole.wait()
-
-
-def update_kernel(dims, pat, values, cols, vh, vl, fix, out):
+
+
+def update_kernel(dims, pat, flags, values, cols, vh, vl, fix, out, stage, sem):
     nr, nc, width, shift = dims
-    r = pl.program_id(0)
     p = lax.axis_index("prow")
     q = lax.axis_index("pcol")
-    row = r * 8 + p
-    eye = eye_of(width)
-
-    def base(c):
-        on_diag = row == c * 16 + q
-        block = values[0, c] * pat[r * nc + c].astype(jnp.float32)
-        return block + jnp.where(on_diag, shift, 0.0).astype(jnp.float32) * eye
-
-    @pl.when(row == 0)
-    def _():
+
+    def out_copy(r):
+        return pltpu.make_async_copy(stage.at[r % SLOTS], out.at[r], sem.at[r % SLOTS])
+
+    def step(r, carry):
+        slot = r % SLOTS
+        row = r * 8 + p
+
+        @pl.when(r >= SLOTS)
+        def _():
+            out_copy(r - SLOTS).wait()
+
         for c in range(nc):
-            out[0, c] = base(c)
-
-    @pl.when(row == 1)
-    def _():
-        out[0] = fix[...]
-
-    @pl.when(row > 1)
-    def _():
-        c0h, c0l = split(cols[0, 0])
-        c1h, c1l = split(cols[1, 0])
-        high = jnp.concatenate([c0h, c1h], axis=1)
-        low = jnp.concatenate([c0l, c1l], axis=1)
-        for c in range(nc):
-            prod = dot(high, vh[c]) + (dot(high, vl[c]) + dot(low, vh[c]))
-            keep = base(c)
+            keep = pat[r * nc + c].astype(jnp.float32)
             if c == 0:
-                keep = jnp.where(q < 2, 0.0, 1.0).astype(jnp.float32) * keep
-            out[0, c] = keep - prod
+                keep = jnp.where((q < 2) & (row > 1), 0.0, keep)
+            stage[slot, c] = values[r, c] * keep
+
+            @pl.when(row == c * 16 + q)
+            def _():
+                stage[slot, c] += shift * eye_of(width)
+
+        def subtract(part):
+            high, low = split(part())
+            rows = {2: slice(0, 2 * width), 0: slice(0, width), 1: slice(width, 2 * width)}[part.which]
+            for c in range(nc):
+                prod = dot(high, vh[c, rows]) + (dot(high, vl[c, rows]) + dot(low, vh[c, rows]))
+                stage[slot, c] -= prod
+
+        first = flags[r] > 0
+        second = flags[nr + r] > 0
+        trail = row > 1
+
+        def both():
+            return jnp.concatenate([cols[0, r], cols[1, r]], axis=1)
+
+        def only_first():
+            return cols[0, r]
+
+        def only_second():
+            return cols[1, r]
+
+        both.which, only_first.which, only_second.which = 2, 0, 1
+        pl.when(trail & first & second)(lambda: subtract(both))
+        pl.when(trail & first & jnp.logical_not(second))(lambda: subtract(only_first))
+        pl.when(trail & jnp.logical_not(first) & second)(lambda: subtract(only_second))
+
+        @pl.when(row == 1)
+        def _():
+            stage[slot] = fix[...]
+
+        out_copy(r).start()
+        return carry
+
+    lax.fori_loop(0, nr, step, 0)
+    for r in range(nr - SLOTS, nr):
+        out_copy(r).wait()
 
 
 def body(values, pattern):
@@ -402,25 +467,30 @@
     f32, bf16 = jnp.float32, jnp.bfloat16
     vmem = pl.BlockSpec(memory_space=pltpu.VMEM)
     dma = pltpu.SemaphoreType.DMA
-    cols, vh, vl, fix = pl.pallas_call(
+    smem = pl.BlockSpec(memory_space=pltpu.SMEM)
+    anywhere = pl.BlockSpec(memory_space=pl.ANY)
+    *held, flags = pl.pallas_call(
         functools.partial(comm_kernel, dims),
         out_shape=(
-            jax.ShapeDtypeStruct((2, nr, width, width), f32),
-            jax.ShapeDtypeStruct((nc, 2 * width, width), bf16),
-            jax.ShapeDtypeStruct((nc, 2 * width, width), bf16),
-            jax.ShapeDtypeStruct((nc, width, width), f32),
+            pltpu.VMEM((2, nr, width, width), f32),
+            pltpu.VMEM((nr, nc, width, width), f32),
+            pltpu.VMEM((nc, 2 * width, width), bf16),
+            pltpu.VMEM((nc, 2 * width, width), bf16),
+            pltpu.VMEM((nc, width, width), f32),
+            jax.ShapeDtypeStruct((2 * nr,), f32),
         ),
-        in_specs=[pl.BlockSpec(memory_space=pltpu.SMEM), pl.BlockSpec(memory_space=pl.ANY)],
-        out_specs=(pl.BlockSpec(memory_space=pl.ANY), vmem, vmem, vmem),
+        in_specs=[smem, anywhere],
+        out_specs=(vmem, vmem, vmem, vmem, vmem, smem),
         scratch_shapes=[
-            pltpu.VMEM((2, nr, width, width), f32),
             pltpu.VMEM((2, nc, width, width), f32),
             pltpu.VMEM((2, 2, width, width), f32),
             pltpu.VMEM((2, nc, width, width), f32),
             pltpu.VMEM((5, width, width), f32),
+            dma((nr,)),
             dma((nr + nc,)),
-            dma((NT, 2)),
-            dma((NT, nr)),
+            dma((NC_TREES, nr * NT // NC_TREES)),
+            dma((NC_TREES, 2)),
+            dma((NC_TREES, nr * NT // NC_TREES)),
             dma((2, NT, 2)),
             dma((2, NT, nc)),
             dma((2, NT, 2)),
@@ -429,31 +499,22 @@
             dma((nr,)),
             dma((2,)),
             dma((2, NT)),
-            dma,
         ],
         compiler_params=pltpu.CompilerParams(
             collective_id=0, has_side_effects=True, vmem_limit_bytes=40 << 20
         ),
         name="gather_panels",
     )(pat, vals)
-    whole = lambda *shape: pl.BlockSpec(shape, lambda r: (0,) * len(shape))
+    cols, own, vh, vl, fix = [pltpu.with_memory_space_constraint(x, pltpu.VMEM) for x in held]
     out = pl.pallas_call(
         functools.partial(update_kernel, dims),
-        grid=(nr,),
         out_shape=jax.ShapeDtypeStruct((nr, nc, width, width), f32),
-        in_specs=[
-            pl.BlockSpec(memory_space=pltpu.SMEM),
-            pl.BlockSpec((1, nc, width, width), lambda r: (r, 0, 0, 0)),
-            pl.BlockSpec((2, 1, width, width), lambda r: (0, r, 0, 0)),
-            whole(nc, 2 * width, width),
-            whole(nc, 2 * width, width),
-            whole(nc, width, width),
-        ],
-        out_specs=pl.BlockSpec((1, nc, width, width), lambda r: (r, 0, 0, 0)),
+        in_specs=[smem, smem, vmem, vmem, vmem, vmem, vmem],
+        out_specs=anywhere,
+        scratch_shapes=[pltpu.VMEM((SLOTS, nc, width, width), f32), dma((SLOTS,))],
         compiler_params=pltpu.CompilerParams(vmem_limit_bytes=40 << 20),
-        cost_estimate=pl.CostEstimate(flops=6 * nr * nc * width**3 * 2, bytes_accessed=35 << 20, transcendentals=0),
         name="update_blocks",
-    )(pat, vals, cols, vh, vl, fix)
+    )(pat, flags, own, cols, vh, vl, fix)
     return out.reshape(values.shape)
 
 

time: 101 us -> 82.3 us (0.81)
  the two profiles are of different devices: /device:TPU:7 before, /device:TPU:66 now
where the time goes in v2:
time: 82.3 us; the launch traced here: 82.2 us
  Pallas kernels  80.8 us (98%)
  local copies, waits for them, and re-layouts  1.36 us (2%)
    pallas_call x1, Pallas kernels, body(): pl.pallas_call(functools.partial(comm_kernel, dims), out_shape=(pltpu.VME...  69.6 us
    pallas_call x1, Pallas kernels, body(): pl.pallas_call(functools.partial(update_kernel, dims), out_shape=jax.Shap...  11.3 us

profile of v2, /device:TPU:66, one launch (start us, length us, event | category | flops | bytes accessed | tf_op | source)
XLA Modules:
  0.0 82.2 jit_solution(15974666309459398764)
XLA Ops:
  0.0 0.8 copy.5
  0.8 0.6 reshape.9.pat
  1.4 69.6 %gather_panels.1 = (f32[2,12,256,256]{3,2,1,0:T(8,128)S(1)}, f32[12,4,256,256]{3,2,1,0:T(8,128)S(1)}, bf16[4,512,256]{2,1,0:T(8,128)(2,1)S(1)}, bf16[4,512,256]{...) custom-call(s32[48]{0:T(128)} %reshape.9.pat, f32[12,4,256,256]{3,2,1,0:T(8,128)} %bitcast.6), custom_call_target="tpu_custom_call" | custom-call | tf_op jit(solution)/shard_map/gather_panels/pallas_call | solution.py:472
  70.9 11.3 %update_blocks.1 = f32[12,4,256,256]{3,2,1,0:T(8,128)} custom-call(s32[48]{0:T(128)} %reshape.9.pat, f32[24]{0:T(128)} %get-tuple-element.11.flags, f32[12,4,256,256]{3,2,1,0:T(8,128)S(1)} %get-tuple-element.12.values, f32[2,12,256,256]{3,2,1,0:T(8,128)S(1)} %get-tuple-element.13.cols, bf16[4,512,256]{2,1,0:T(8,128)(2,1)S(1)} %get-tuple-element.14.vh, ...), custom_call_target="tpu_custom_call" | custom-call | tf_op jit(solution)/shard_map/update_blocks/pallas_call | solution.py:509

commit v3 on v2

v3 whole, which is shorter than its diff:
```python
import functools
import math

import jax
import jax.numpy as jnp
from jax import lax
from jax.experimental import pallas as pl
from jax.experimental.pallas import tpu as pltpu
from jax.sharding import PartitionSpec as P

SWEEPS = 3
SHIFT_COEF = 5.0
MESH = pl.DeviceIdType.MESH

COL_TREES = (
    ((0, 0, 1, 0), (1, 0, 2, 0), (1, 0, 1, 1), (2, 0, 3, 0), (2, 0, 2, 1), (1, 1, 0, 1), (2, 1, 3, 1)),
    ((0, 0, 3, 0), (3, 0, 2, 0), (3, 0, 3, 1), (2, 0, 1, 0), (3, 1, 2, 1), (3, 1, 0, 1), (2, 1, 1, 1)),
    ((0, 0, 0, 1), (0, 1, 1, 1), (0, 1, 3, 1), (1, 1, 2, 1), (1, 1, 1, 0), (3, 1, 3, 0), (2, 1, 2, 0)),
)
NC_TREES = len(COL_TREES)
TREES = (
    ((0, 0, 1, 0), (1, 0, 2, 0), (1, 0, 1, 1), (2, 0, 3, 0), (1, 1, 2, 1), (1, 1, 0, 1), (2, 1, 3, 1)),
    ((0, 0, 3, 0), (3, 0, 2, 0), (3, 0, 3, 1), (2, 0, 1, 0), (3, 1, 2, 1), (3, 1, 0, 1), (2, 1, 1, 1)),
    ((0, 0, 1, 0), (1, 0, 2, 0), (2, 0, 3, 0), (2, 0, 2, 1), (2, 1, 3, 1), (2, 1, 1, 1), (3, 1, 0, 1)),
    ((0, 0, 3, 0), (0, 0, 0, 1), (3, 0, 2, 0), (0, 1, 1, 1), (0, 1, 3, 1), (2, 0, 1, 0), (1, 1, 2, 1)),
)
NT = len(TREES)
HOP = 4
ROW_HOP = 2
ROW_STEP = 3
PACE = 4
XS = 4
OWN_AT = 3
SLOTS = 3


def tree_depths(edges):
    depth = {(0, 0): 0}
    for a, b, c, d in edges:
        depth[c, d] = depth[a, b] + 1
    return depth


COL_DEPTHS = tuple(tree_depths(edges) for edges in COL_TREES)
DEPTHS = tuple(tree_depths(edges) for edges in TREES)
COL_DEPTH = max(max(d.values()) for d in COL_DEPTHS)
ROW_DEPTH = max(max(d.values()) for d in DEPTHS)


def lookup(node, table):
    out = jnp.int32(0)
    for (a, b), value in table.items():
        if value:
            out = jnp.where(node == a * 2 + b, jnp.int32(value), out)
    return out


def split(x):
    high = x.astype(jnp.bfloat16)
    return high, (x - high.astype(jnp.float32)).astype(jnp.bfloat16)


def dot(a, b):
    return jnp.dot(a, b, preferred_element_type=jnp.float32)


def mm(a, b):
    ah, al = split(a)
    bh, bl = split(b)
    return dot(ah, bh) + (dot(ah, bl) + dot(al, bh))


def eye_of(width):
    rows = lax.broadcasted_iota(jnp.int32, (width, width), 0)
    cols = lax.broadcasted_iota(jnp.int32, (width, width), 1)
    return jnp.where(rows == cols, 1.0, 0.0).astype(jnp.float32)


def comm_kernel(
    dims, pat, values, colbuf, own, vh_out, vl_out, fix_out, flags,
    rowbuf, vtmp, xs,
    own_sem, load_sem, root_sem, col_send, col_recv, sib_send, sib_recv,
    row_send, row_recv, src_send, src_recv, give_send, give_recv,
    x_send, x_recv, xs_send, xs_recv, xsib_send, xsib_recv,
):
    nr, nc, width, shift = dims
    qr = width // NT
    chunks = nr * NT // NC_TREES
    p = lax.axis_index("prow")
    q = lax.axis_index("pcol")
    xlo, z = p // 4, p % 4
    y, xhi, core = q // 4, (q // 2) % 2, q % 2

    def dev(xlo_, z_, y_, xhi_, core_):
        return (xlo_ * 4 + z_, y_ * 4 + xhi_ * 2 + core_)

    sibling = dev(xlo, z, y, xhi, 1 - core)
    barrier = pltpu.get_barrier_semaphore()
    partners = (
        sibling,
        dev(xlo, z, (y + 1) % 4, xhi, core),
        dev(xlo, z, (y + 3) % 4, xhi, core),
        dev(xlo, z, y, 1 - xhi, core),
        dev(xlo, (z + 1) % 4, y, xhi, core),
        dev(xlo, (z + 3) % 4, y, xhi, core),
        dev(1 - xlo, z, y, xhi, core),
    )
    for partner in partners:
        pl.semaphore_signal(barrier, inc=1, device_id=partner, device_id_type=MESH)

    cnode = y * 2 + xhi
    cdepth = [lookup(cnode, d) for d in COL_DEPTHS]
    rnode = [((z + 4 - k) % 4) * 2 + xlo for k in range(2)]
    rdepth = [[lookup(rnode[k], d) for d in DEPTHS] for k in range(2)]

    def children(edges, node, place):
        kids = {}
        for a, b, c, d in edges:
            kids.setdefault((a, b), []).append((c, d))
        out = []
        for slot in range(max(len(v) for v in kids.values())):
            has = {n: 1 for n, v in kids.items() if len(v) > slot}
            to_a = lookup(node, {n: v[slot][0] for n, v in kids.items() if len(v) > slot})
            to_b = lookup(node, {n: v[slot][1] for n, v in kids.items() if len(v) > slot})
            out.append((lookup(node, has) == 1, place(to_a, to_b)))
        return out

    ckids = [children(e, cnode, lambda a, b: dev(xlo, z, a, b, core)) for e in COL_TREES]
    rkids = [
        [children(e, rnode[k], lambda a, b, k=k: dev(b, (a + k) % 4, y, xhi, core)) for e in TREES]
        for k in range(2)
    ]

    def remote(src, dst, send, recv, device):
        return pltpu.make_async_remote_copy(
            src_ref=src, dst_ref=dst, send_sem=send, recv_sem=recv,
            device_id=device, device_id_type=MESH,
        )

    def arrive(ref, sem):
        pltpu.make_async_copy(ref, ref, sem).wait()

    eye = eye_of(width)
    col_root = cnode == 0
    row_root = [p == k for k in range(2)]
    column_core, row_core = core == 0, core == 1

    def block_of(n, t):
        return NC_TREES * (n // NT) + t

    def col_chunk(j, t, n):
        return colbuf.at[j, block_of(n, t), pl.ds((n % NT) * qr, qr)]

    def send_col(j, t, n):
        ref = col_chunk(j, t, n)
        for slot, (has, device) in enumerate(ckids[t]):
            pl.when(has)(remote(ref, ref, col_send.at[j, t, slot], col_recv.at[j, t, n], device).start)

    def root_send(j, t, n):
        ref = col_chunk(j, t, n)
        return remote(ref, ref, root_sem.at[j, t, n], col_recv.at[j, t, n], ckids[t][0][1])

    def sib_copy(j, u):
        ref = colbuf.at[j, u]
        return remote(ref, ref, sib_send.at[j], sib_recv.at[j, u], sibling)

    def send_row(k, t, v):
        for h in range(2):
            ref = rowbuf.at[k, h, v, pl.ds(t * qr, qr)]
            for slot, (has, device) in enumerate(rkids[k][t]):
                sems = row_send.at[k, h, t, slot], row_recv.at[k, h, t, v]
                pl.when(has)(remote(ref, ref, *sems, device).start)

    def xs_chunk(m):
        return xs.at[m // NT, pl.ds((m % NT) * qr, qr)]

    def send_xs(t, m):
        ref = xs_chunk(m)
        for slot, (has, device) in enumerate(ckids[t]):
            pl.when(has)(remote(ref, ref, xs_send.at[t, slot], xs_recv.at[m], device).start)

    def src_copy(k, v):
        ref = rowbuf.at[k, 0, v]
        return remote(ref, ref, src_send.at[k], src_recv.at[k, v], sibling)

    def give_copy(k, t):
        ref = rowbuf.at[k, 0, pl.ds(0, nc), pl.ds(t * qr, qr)]
        return remote(ref, ref, give_send.at[k], give_recv.at[k, t], sibling)

    def x_copy(i):
        ref = xs.at[i]
        return remote(ref, ref, x_send.at[i], x_recv.at[i], sibling)

    def load_col(u):
        return pltpu.make_async_copy(values.at[u, 0], colbuf.at[core, u], load_sem.at[u])

    def load_row(k, v):
        return pltpu.make_async_copy(values.at[0, v], rowbuf.at[k, core, v], load_sem.at[nr + v])

    def load_own(u):
        return pltpu.make_async_copy(values.at[u], own.at[u], own_sem.at[u])

    def ready_col(u):
        load_col(u).wait()
        on_diag = (u == 0) & (p == core)
        block = colbuf[core, u] * pat[u * nc].astype(jnp.float32)
        colbuf[core, u] = block + jnp.where(on_diag, shift, 0.0).astype(jnp.float32) * eye

    def ready_own(u):
        load_own(u).wait()
        row = u * 8 + p
        for c in range(nc):
            keep = pat[u * nc + c].astype(jnp.float32)
            if c == 0:
                keep = jnp.where((q < 2) & (row > 1), 0.0, keep)
            own[u, c] = own[u, c] * keep

            @pl.when(row == c * 16 + q)
            def _():
                own[u, c] += shift * eye

    @pl.when(col_root)
    def _():
        for u in range(nr):
            load_col(u).start()

    for k in range(2):
        @pl.when(row_root[k])
        def _():
            for v in range(nc):
                load_row(k, v).start()

    for u in range(nr):
        load_own(u).start()

    pl.semaphore_wait(barrier, len(partners))

    @pl.when(col_root & row_core)
    def _():
        def one(u, carry):
            ready_col(u)
            sib_copy(1, u).start()
            return carry

        lax.fori_loop(0, nr, one, 0)

    for k in range(2):
        @pl.when(row_root[k])
        def _():
            for v in range(nc):
                load_row(k, v).wait()
                block = rowbuf[k, core, v] * pat[v].astype(jnp.float32)
                if v == 0:
                    block = block + jnp.where(q == k, shift, 0.0).astype(jnp.float32) * eye
                rowbuf[k, core, v] = block

                @pl.when(column_core)
                def _():
                    src_copy(k, v).start()

    def mark(j, u):
        flags[j * nr + u] = jnp.max(jnp.abs(colbuf[j, u]))

    xs_count = XS * NT
    xs_rounds = -(-xs_count // NC_TREES)

    def col_step(s, carry):
        pl.when((s >= OWN_AT) & (s < OWN_AT + nr))(lambda: ready_own(s - OWN_AT))
        for t in range(NC_TREES):
            n = s - HOP * cdepth[t]
            m = (n - chunks) * NC_TREES + t

            @pl.when((n >= chunks) & (m < xs_count))
            def _():
                @pl.when(cdepth[t] > 0)
                def _():
                    arrive(xs_chunk(m), xs_recv.at[m])

                if t == 0:
                    @pl.when((cdepth[t] == 0) & (n == chunks))
                    def _():
                        for i in range(XS):
                            arrive(xs.at[i], x_recv.at[i])

                send_xs(t, m)

                @pl.when(cdepth[t] > 0)
                def _():
                    ref = xs_chunk(m)
                    remote(ref, ref, xsib_send, xsib_recv.at[m], sibling).start()

            @pl.when((n >= 0) & (n < chunks))
            def _():
                u = block_of(n, t)
                for j in range(2):
                    @pl.when(cdepth[t] > 0)
                    def _():
                        arrive(col_chunk(j, t, n), col_recv.at[j, t, n])
                        send_col(j, t, n)

                        @pl.when(n % NT == NT - 1)
                        def _():
                            sib_copy(j, u).start()
                            mark(j, u)

                    @pl.when(cdepth[t] == 0)
                    def _():
                        @pl.when(n % NT == 0)
                        def _():
                            if j == 0:
                                ready_col(u)
                                sib_copy(0, u).start()
                            else:
                                arrive(colbuf.at[1, u], sib_recv.at[1, u])
                            mark(j, u)

                        @pl.when(n >= PACE)
                        def _():
                            root_send(j, t, n - PACE).wait_send()

                        root_send(j, t, n).start()

        return carry

    def newton_steps(block_ref, out):
        def first():
            block = block_ref[...]
            xs[out] = (2.0 * eye - block * (1.0 / shift)) * (1.0 / shift)

        def inner():
            xs[5] = 2.0 * eye - mm(block_ref[...], xs[out])

        def outer():
            xs[out] = mm(xs[out], xs[5])

        steps = [first]
        for _ in range(SWEEPS - 1):
            steps += [inner, outer]
        return steps

    def middle():
        xs[2] = mm(rowbuf[1, 0, 0], xs[0])

    def schur():
        xs[4] = rowbuf[1, 1, 0] - mm(xs[2], rowbuf[0, 1, 0])

    def corner():
        xs[3] = rowbuf[0, 1, 0]
        x_copy(3).start()

    work = [corner]
    work += newton_steps(rowbuf.at[0, 0, 0], 0)
    work += [x_copy(0).start, middle, x_copy(2).start, schur]
    work += newton_steps(xs.at[4], 1)
    work += [x_copy(1).start]

    work_at = ROW_HOP * ROW_DEPTH
    row_last = ROW_STEP * (nc - 1) + ROW_HOP * ROW_DEPTH + 1
    per = len(work)

    def row_step(s, carry):
        pl.when((s >= OWN_AT) & (s < OWN_AT + nr))(lambda: ready_own(s - OWN_AT))
        for k in range(2):
            for t in range(NT):
                w = s - ROW_HOP * rdepth[k][t]
                for v in range(nc):
                    @pl.when(w == ROW_STEP * v)
                    def _():
                        @pl.when(rdepth[k][t] == 0)
                        def _():
                            if t == 0:
                                arrive(rowbuf.at[k, 0, v], src_recv.at[k, v])

                        @pl.when(rdepth[k][t] > 0)
                        def _():
                            for h in range(2):
                                ref = rowbuf.at[k, h, v, pl.ds(t * qr, qr)]
                                arrive(ref, row_recv.at[k, h, t, v])

                        send_row(k, t, v)
                        if v == nc - 1:
                            @pl.when(rdepth[k][t] > 0)
                            def _():
                                give_copy(k, t).start()

        for i in range(row_last - work_at):
            part = work[i * per:(i + 1) * per]
            if part:
                @pl.when(col_root & (s == work_at + i))
                def _():
                    for item in part:
                        item()
        return carry

    @pl.when(column_core)
    def _():
        lax.fori_loop(0, chunks + xs_rounds + HOP * COL_DEPTH, col_step, 0)
        for k in range(2):
            @pl.when(jnp.logical_not(row_root[k]))
            def _():
                for t in range(NT):
                    ref = rowbuf.at[k, 0, pl.ds(0, nc), pl.ds(t * qr, qr)]
                    arrive(ref, give_recv.at[k, t])

    @pl.when(row_core)
    def _():
        lax.fori_loop(0, row_last, row_step, 0)

        def have(u, carry):
            arrive(colbuf.at[0, u], sib_recv.at[0, u])
            pl.when(jnp.logical_not(col_root))(functools.partial(arrive, colbuf.at[1, u], sib_recv.at[1, u]))
            for j in range(2):
                mark(j, u)
            return carry

        lax.fori_loop(0, nr, have, 0)

        @pl.when(jnp.logical_not(col_root))
        def _():
            for m in range(xs_count):
                arrive(xs_chunk(m), xsib_recv.at[m])

    def put_v(k, c, value):
        high, low = split(value)
        vh_out[c, pl.ds(k * width, width)] = high
        vl_out[c, pl.ds(k * width, width)] = low

    def solve(c):
        upper = rowbuf[0, core, c]
        vtmp[1, c] = rowbuf[1, core, c] - mm(xs[2], upper)

        @pl.when(p == 1)
        def _():
            fix_out[c] = vtmp[1, c]

            if c == 0:
                @pl.when(q == 0)
                def _():
                    fix_out[0] = xs[2]

        if c == 0:
            @pl.when(q < 2)
            def _():
                vtmp[1, 0] = jnp.where(q == 1, -1.0, 0.0).astype(jnp.float32) * eye

            upper = jnp.where(q < 2, jnp.where(q == 0, -1.0, 0.0).astype(jnp.float32) * eye, upper)
        vtmp[0, c] = upper

    for c in range(nc):
        solve(c)
    for c in range(nc):
        value = mm(xs[1], vtmp[1, c])
        vtmp[1, c] = value
        put_v(1, c, value)
    for c in range(nc):
        vtmp[0, c] = vtmp[0, c] - mm(xs[3], vtmp[1, c])
    for c in range(nc):
        put_v(0, c, mm(xs[0], vtmp[0, c]))

    @pl.when(column_core)
    def _():
        for j in range(2):
            for t in range(NC_TREES):
                for slot, (has, _) in enumerate(ckids[t]):
                    ref = colbuf.at[0, pl.ds(0, nr // NC_TREES)]
                    pl.when(has & (cnode > 0))(functools.partial(arrive, ref, col_send.at[j, t, slot]))

                @pl.when(col_root)
                def _():
                    for n in range(chunks - PACE, chunks):
                        root_send(j, t, n).wait_send()

            sent = jnp.logical_not(col_root) if j == 1 else (p >= 0)
            pl.when(sent)(functools.partial(arrive, colbuf.at[0], sib_send.at[j]))
        for t in range(NC_TREES):
            sent = len(range(t, xs_count, NC_TREES))
            for slot, (has, _) in enumerate(ckids[t]):
                ref = colbuf.at[0, pl.ds(0, sent), pl.ds(0, qr)]
                pl.when(has)(functools.partial(arrive, ref, xs_send.at[t, slot]))
        given = jnp.logical_not(col_root)
        pl.when(given)(functools.partial(arrive, xs.at[pl.ds(0, XS)], xsib_send))
        for k in range(2):
            pl.when(row_root[k])(functools.partial(arrive, rowbuf.at[0, 0], src_send.at[k]))

    @pl.when(row_core)
    def _():
        for k in range(2):
            for t in range(NT):
                for h in range(2):
                    for slot, (has, _) in enumerate(rkids[k][t]):
                        ref = rowbuf.at[0, 0, pl.ds(0, nc), pl.ds(0, qr)]
                        pl.when(has)(functools.partial(arrive, ref, row_send.at[k, h, t, slot]))
            given = jnp.logical_not(row_root[k])
            pl.when(given)(functools.partial(arrive, rowbuf.at[0, 0], give_send.at[k]))
        pl.when(col_root)(functools.partial(arrive, colbuf.at[0], sib_send.at[1]))

        @pl.when(col_root)
        def _():
            for i in range(XS):
                x_copy(i).wait_send()


def update_kernel(dims, flags, own, cols, vh, vl, fix, out, stage, sem):
    nr, nc, width, shift = dims
    p = lax.axis_index("prow")

    def out_copy(r, source):
        return pltpu.make_async_copy(source, out.at[r], sem.at[r % SLOTS])

    def step(r, carry):
        slot = r % SLOTS
        row = r * 8 + p

        @pl.when(r >= SLOTS)
        def _():
            out_copy(r - SLOTS, stage.at[slot]).wait()

        def subtract(left, rows):
            high, low = split(left)
            for c in range(nc):
                prod = dot(high, vh[c, rows]) + (dot(high, vl[c, rows]) + dot(low, vh[c, rows]))
                stage[slot, c] = own[r, c] - prod
            out_copy(r, stage.at[slot]).start()

        first = flags[r] > 0
        second = flags[nr + r] > 0
        trail = row > 1
        both = trail & first & second
        only_first = trail & first & jnp.logical_not(second)
        only_second = trail & jnp.logical_not(first) & second
        kept = (row == 0) | (trail & jnp.logical_not(first) & jnp.logical_not(second))

        @pl.when(both)
        def _():
            subtract(jnp.concatenate([cols[0, r], cols[1, r]], axis=1), slice(0, 2 * width))

        @pl.when(only_first)
        def _():
            subtract(cols[0, r], slice(0, width))

        @pl.when(only_second)
        def _():
            subtract(cols[1, r], slice(width, 2 * width))

        pl.when(kept)(lambda: out_copy(r, own.at[r]).start())
        pl.when(row == 1)(lambda: out_copy(r, fix).start())
        return carry

    lax.fori_loop(0, nr, step, 0)
    for r in range(nr - SLOTS, nr):
        out_copy(r, stage.at[r % SLOTS]).wait()


def body(values, pattern):
    nr, _, nc, _, width, _ = values.shape
    shift = SHIFT_COEF * math.sqrt(width)
    dims = (nr, nc, width, shift)
    vals = values.reshape(nr, nc, width, width)
    pat = pattern.reshape(nr * nc)
    f32, bf16 = jnp.float32, jnp.bfloat16
    vmem = pl.BlockSpec(memory_space=pltpu.VMEM)
    dma = pltpu.SemaphoreType.DMA
    smem = pl.BlockSpec(memory_space=pltpu.SMEM)
    anywhere = pl.BlockSpec(memory_space=pl.ANY)
    *held, flags = pl.pallas_call(
        functools.partial(comm_kernel, dims),
        out_shape=(
            pltpu.VMEM((2, nr, width, width), f32),
            pltpu.VMEM((nr, nc, width, width), f32),
            pltpu.VMEM((nc, 2 * width, width), bf16),
            pltpu.VMEM((nc, 2 * width, width), bf16),
            pltpu.VMEM((nc, width, width), f32),
            jax.ShapeDtypeStruct((2 * nr,), f32),
        ),
        in_specs=[smem, anywhere],
        out_specs=(vmem, vmem, vmem, vmem, vmem, smem),
        scratch_shapes=[
            pltpu.VMEM((2, 2, nc, width, width), f32),
            pltpu.VMEM((2, nc, width, width), f32),
            pltpu.VMEM((6, width, width), f32),
            dma((nr,)),
            dma((nr + nc,)),
            dma((2, NC_TREES, nr * NT // NC_TREES)),
            dma((2, NC_TREES, 2)),
            dma((2, NC_TREES, nr * NT // NC_TREES)),
            dma((2,)),
            dma((2, nr)),
            dma((2, 2, NT, 2)),
            dma((2, 2, NT, nc)),
            dma((2,)),
            dma((2, nc)),
            dma((2,)),
            dma((2, NT)),
            dma((XS,)),
            dma((XS,)),
            dma((NC_TREES, 2)),
            dma((XS * NT,)),
            dma,
            dma((XS * NT,)),
        ],
        compiler_params=pltpu.CompilerParams(
            collective_id=0, has_side_effects=True, vmem_limit_bytes=40 << 20
        ),
        name="gather_panels",
    )(pat, vals)
    cols, own, vh, vl, fix = [pltpu.with_memory_space_constraint(x, pltpu.VMEM) for x in held]
    out = pl.pallas_call(
        functools.partial(update_kernel, dims),
        out_shape=jax.ShapeDtypeStruct((nr, nc, width, width), f32),
        in_specs=[smem, vmem, vmem, vmem, vmem, vmem],
        out_specs=anywhere,
        scratch_shapes=[pltpu.VMEM((SLOTS, nc, width, width), f32), dma((SLOTS,))],
        compiler_params=pltpu.CompilerParams(vmem_limit_bytes=40 << 20),
        name="update_blocks",
    )(flags, own, cols, vh, vl, fix)
    return out.reshape(values.shape)


def solution(mesh):
    return jax.shard_map(
        body,
        mesh=mesh,
        in_specs=(P(None, "prow", None, "pcol", None, None), P(None, "prow", None, "pcol")),
        out_specs=P(None, "prow", None, "pcol", None, None),
        check_vma=False,
    )
```

time: 82.3 us -> 77.8 us (0.945)
  the two profiles are of different devices: /device:TPU:66 before, /device:TPU:49 now
where the time goes in v3:
time: 77.8 us; the launch traced here: 77.7 us
  Pallas kernels  76.4 us (98%)
  local copies, waits for them, and re-layouts  1.37 us (2%)
    pallas_call x1, Pallas kernels, body(): pl.pallas_call(functools.partial(comm_kernel, dims), out_shape=(pltpu.VME...  67.6 us
    pallas_call x1, Pallas kernels, body(): pl.pallas_call(functools.partial(update_kernel, dims), out_shape=jax.Shap...  8.77 us

profile of v3, /device:TPU:49, one launch (start us, length us, event | category | flops | bytes accessed | tf_op | source)
XLA Modules:
  0.0 77.7 jit_solution(598559180947329680)
XLA Ops:
  0.0 0.8 copy.5
  0.8 0.6 reshape.9.pat
  1.4 67.6 %gather_panels.1 = (f32[2,12,256,256]{3,2,1,0:T(8,128)S(1)}, f32[12,4,256,256]{3,2,1,0:T(8,128)S(1)}, bf16[4,512,256]{2,1,0:T(8,128)(2,1)S(1)}, bf16[4,512,256]{...) custom-call(s32[48]{0:T(128)} %reshape.9.pat, f32[12,4,256,256]{3,2,1,0:T(8,128)} %bitcast.6), custom_call_target="tpu_custom_call" | custom-call | tf_op jit(solution)/shard_map/gather_panels/pallas_call | solution.py:565
  69.0 8.8 %update_blocks.1 = f32[12,4,256,256]{3,2,1,0:T(8,128)} custom-call(f32[24]{0:T(128)} %get-tuple-element.11.flags, f32[12,4,256,256]{3,2,1,0:T(8,128)S(1)} %get-tuple-element.12.own, f32[2,12,256,256]{3,2,1,0:T(8,128)S(1)} %get-tuple-element.13.cols, bf16[4,512,256]{2,1,0:T(8,128)(2,1)S(1)} %get-tuple-element.14.vh, ...), custom_call_target="tpu_custom_call" | custom-call | tf_op jit(solution)/shard_map/update_blocks/pallas_call | solution.py:607

commit v4 on v3

--- a/solution.py
+++ b/solution.py
@@ -31,7 +31,7 @@
 PACE = 4
 XS = 4
 OWN_AT = 3
-SLOTS = 3
+SLOTS = 6
 
 
 def tree_depths(edges):
@@ -354,9 +354,10 @@
     work += newton_steps(xs.at[4], 1)
     work += [x_copy(1).start]
 
-    work_at = ROW_HOP * ROW_DEPTH
+    deepest = rdepth[0][0]
+    for d in rdepth[0] + rdepth[1]:
+        deepest = jnp.maximum(deepest, d)
     row_last = ROW_STEP * (nc - 1) + ROW_HOP * ROW_DEPTH + 1
-    per = len(work)
 
     def row_step(s, carry):
         pl.when((s >= OWN_AT) & (s < OWN_AT + nr))(lambda: ready_own(s - OWN_AT))
@@ -383,13 +384,11 @@
                             def _():
                                 give_copy(k, t).start()
 
-        for i in range(row_last - work_at):
-            part = work[i * per:(i + 1) * per]
-            if part:
-                @pl.when(col_root & (s == work_at + i))
-                def _():
-                    for item in part:
-                        item()
+        @pl.when(col_root & (s == ROW_HOP * deepest))
+        def _():
+            for item in work:
+                item()
+
         return carry
 
     @pl.when(column_core)

time: 77.8 us -> 77.7 us (level)
  no operation moved by 1% of the time
where the time goes in v4:
time: 77.7 us; the launch traced here: 77.2 us
  Pallas kernels  75.9 us (98%)
  local copies, waits for them, and re-layouts  1.37 us (2%)
    pallas_call x1, Pallas kernels, body(): pl.pallas_call(functools.partial(comm_kernel, dims), out_shape=(pltpu.VME...  67.6 us
    pallas_call x1, Pallas kernels, body(): pl.pallas_call(functools.partial(update_kernel, dims), out_shape=jax.Shap...  8.26 us

profile of v4, /device:TPU:49, one launch (start us, length us, event | category | flops | bytes accessed | tf_op | source)
XLA Modules:
  0.0 77.2 jit_solution(6799773962114045090)
XLA Ops:
  0.0 0.8 copy.5
  0.8 0.6 reshape.9.pat
  1.4 67.6 %gather_panels.1 = (f32[2,12,256,256]{3,2,1,0:T(8,128)S(1)}, f32[12,4,256,256]{3,2,1,0:T(8,128)S(1)}, bf16[4,512,256]{2,1,0:T(8,128)(2,1)S(1)}, bf16[4,512,256]{...) custom-call(s32[48]{0:T(128)} %reshape.9.pat, f32[12,4,256,256]{3,2,1,0:T(8,128)} %bitcast.6), custom_call_target="tpu_custom_call" | custom-call | tf_op jit(solution)/shard_map/gather_panels/pallas_call | solution.py:564
  69.0 8.3 %update_blocks.1 = f32[12,4,256,256]{3,2,1,0:T(8,128)} custom-call(f32[24]{0:T(128)} %get-tuple-element.11.flags, f32[12,4,256,256]{3,2,1,0:T(8,128)S(1)} %get-tuple-element.12.own, f32[2,12,256,256]{3,2,1,0:T(8,128)S(1)} %get-tuple-element.13.cols, bf16[4,512,256]{2,1,0:T(8,128)(2,1)S(1)} %get-tuple-element.14.vh, ...), custom_call_target="tpu_custom_call" | custom-call | tf_op jit(solution)/shard_map/update_blocks/pallas_call | solution.py:606
